TPU v7x, 128 devices: a whole 4x4x4 slice. The times are simulated.
128 devices in a mesh: doc: 2 (over core), head: 2 (over y_lo), seq: 32 (over x, z, y_hi).
Axes of the slice: x: 4, y: 4 (y_hi: 2, y_lo: 2; y = y_hi * 2 + y_lo), z: 4, core: 2. Of those that a mesh axis runs over, the one named last changes fastest.
Arguments:
- token_ids: int32 [2, 16384], P('doc', 'seq'), may hold values from 0 to 152063, as said below
- teacher_query: bfloat16 [2, 16384, 8192], P('doc', 'seq', 'head'), may hold values from -4.5 to 4.5
- teacher_value: bfloat16 [2, 16384, 1024], P('doc', 'seq', 'head'), may hold values from -4.5 to 4.5
- student_query: bfloat16 [2, 16384, 3584], P('doc', 'seq'), may hold values from -4.5 to 4.5
- student_value: bfloat16 [2, 16384, 512], P('doc', 'seq'), may hold values from -4.5 to 4.5
- teacher_pick: int32 [4], replicated, may hold values from 0 to 127
- student_pick: int32 [4], replicated, may hold values from 0 to 55
Outputs:
- grad_query: float32 [2, 16384, 256], P('doc', 'seq', 'head')
- grad_value: float32 [2, 16384, 256], P('doc', 'seq', 'head')
- loss: float32 [2], P('doc')
Inputs may be any that keep to these rules, and one draw needn't show every extreme that they name: `token_ids`: 0 marks padding, which fills the tail of each document and is present in every document; at least half of a document's 16384 tokens are not padding; the first token of every document is the id 152064 - 1.
All inputs are finite; a program needn't handle non-finite values.
Results may differ from a plain program's by a relative error of at most 0.0023.
Values may be sent and summed in bfloat16 or wider, within the bound.
A program may use at most 128 MiB of HBM per device.

v0:
```python
import math

import jax
import jax.numpy as jnp
from jax import lax
from jax.sharding import PartitionSpec as P

T_HEADS = 64
T_KV = 8
S_HEADS = 28
S_KV = 4
HEAD_DIM = 128
REL_HEADS = 4
REL_WIDTH = 64


def shards(
    token_ids,
    teacher_query,
    teacher_value,
    student_query,
    student_value,
    teacher_pick,
    student_pick,
):
    scale = REL_WIDTH ** (-0.5)
    per_head = HEAD_DIM // REL_WIDTH
    my_head = lax.axis_index("head")
    n_head = lax.axis_size("head")
    heads_mine = REL_HEADS // n_head
    half_width = heads_mine * REL_WIDTH
    own_ids = token_ids[0]
    rows = own_ids.shape[0]
    own_live = own_ids != 0

    def local_pick(array, block, local_blocks):
        owner_idx = block // local_blocks
        columns = lax.dynamic_slice_in_dim(array[0], block % local_blocks * REL_WIDTH, REL_WIDTH, 1)
        return jnp.where(owner_idx == my_head, columns, jnp.zeros_like(columns))

    q_blocks = teacher_query.shape[2] // REL_WIDTH
    v_blocks = teacher_value.shape[2] // REL_WIDTH
    query_parts = []
    value_parts = []
    for rel in range(REL_HEADS):
        t_block = teacher_pick[rel]
        t_vblock = t_block // per_head // (T_HEADS // T_KV) * per_head + t_block % per_head
        query_parts.append(local_pick(teacher_query, t_block, q_blocks))
        value_parts.append(local_pick(teacher_value, t_vblock, v_blocks))
    local_sel = jnp.stack([jnp.concatenate(query_parts, 1), jnp.concatenate(value_parts, 1)], 0)
    teach = lax.psum_scatter(
        local_sel.astype(jnp.float32).astype(jnp.bfloat16), "head", scatter_dimension=2, tiled=True
    )
    stud_query_parts = []
    stud_value_parts = []
    for slot in range(heads_mine):
        s_block = student_pick[my_head * heads_mine + slot]
        s_vblock = s_block // per_head // (S_HEADS // S_KV) * per_head + s_block % per_head
        stud_query_parts.append(
            lax.dynamic_slice_in_dim(student_query[0], s_block * REL_WIDTH, REL_WIDTH, 1)
        )
        stud_value_parts.append(
            lax.dynamic_slice_in_dim(student_value[0], s_vblock * REL_WIDTH, REL_WIDTH, 1)
        )
    features = jnp.stack(
        [
            teach[0],
            jnp.concatenate(stud_query_parts, 1),
            teach[1],
            jnp.concatenate(stud_value_parts, 1),
        ],
        1,
    )
    own_five = features.reshape(rows, 2, 2, heads_mine, REL_WIDTH)

    def score_tiles(key_five):
        return (
            jnp.einsum("ikshd,jkshd->kshij", own_five, key_five, preferred_element_type=jnp.float32)
            * scale
        )

    def block_plan(count_rows):
        width = math.gcd(count_rows, 1024)
        return (width, count_rows // width)

    def row_update(states, tiles, alive):
        run_max, run_sum = states
        masked = jnp.where(alive, tiles, -1e30)
        new_max = jnp.maximum(run_max, jnp.max(masked, axis=-1))
        added = jnp.sum(jnp.where(alive, jnp.exp(tiles - new_max[..., None]), 0.0), axis=-1)
        return (new_max, run_sum * jnp.exp(run_max - new_max) + added)

    start_stats = (
        jnp.full((2, 2, heads_mine, rows), -1e30, jnp.float32),
        jnp.zeros((2, 2, heads_mine, rows), jnp.float32),
    )
    whole_feats, whole_ids = (
        lax.all_gather(features, "seq", axis=0, tiled=True),
        lax.all_gather(own_ids, "seq", axis=0, tiled=True),
    )
    width, steps = block_plan(whole_feats.shape[0])

    def first_one_block(step_idx, states):
        sub = lax.dynamic_slice_in_dim(whole_feats, step_idx * width, width, 0).reshape(
            width, 2, 2, heads_mine, REL_WIDTH
        )
        alive = lax.dynamic_slice_in_dim(whole_ids, step_idx * width, width, 0) != 0
        return row_update(states, score_tiles(sub), alive)

    run_max, run_sum = lax.fori_loop(0, steps, first_one_block, start_stats)
    own_lse = run_max + jnp.log(run_sum)
    all_stats = lax.all_gather(jnp.transpose(own_lse, (3, 0, 1, 2)), "seq", axis=0, tiled=True)
    lt_rows = own_lse[:, 0][..., None]
    ls_rows = own_lse[:, 1][..., None]

    def tile_terms(sub, alive, key_stats):
        tiles = score_tiles(sub)
        tile_t = tiles[:, 0]
        tile_s = tiles[:, 1]
        both = own_live[:, None] & alive[None, :]
        diff_rows = jnp.where(both, jnp.exp(tile_s - ls_rows) - jnp.exp(tile_t - lt_rows), 0.0)
        diff_cols = jnp.where(
            both,
            jnp.exp(tile_s - key_stats[:, 1][..., None, :])
            - jnp.exp(tile_t - key_stats[:, 0][..., None, :]),
            0.0,
        )
        weights = (diff_rows + diff_cols).astype(jnp.bfloat16)
        return (tile_t, tile_s, both, weights)

    start_grads = (
        jnp.zeros((2, heads_mine, rows, REL_WIDTH), jnp.float32),
        jnp.zeros((2, heads_mine, rows), jnp.float32),
    )
    second_width, steps = block_plan(whole_feats.shape[0])

    def second_one_block(step_idx, states):
        sub = lax.dynamic_slice_in_dim(
            whole_feats, step_idx * second_width, second_width, 0
        ).reshape(second_width, 2, 2, heads_mine, REL_WIDTH)
        alive = lax.dynamic_slice_in_dim(whole_ids, step_idx * second_width, second_width, 0) != 0
        key_stats = jnp.transpose(
            lax.dynamic_slice_in_dim(all_stats, 0 + step_idx * second_width, second_width, 0),
            (1, 2, 3, 0),
        )
        grad_acc, kl_acc = states
        tile_t, tile_s, both, weights = tile_terms(sub, alive, key_stats)
        grad_acc = (
            grad_acc
            + jnp.einsum(
                "khij,jkhd->khid", weights, sub[:, :, 1], preferred_element_type=jnp.float32
            )
            * scale
        )
        kl_acc = kl_acc + jnp.sum(
            jnp.where(both, jnp.exp(tile_t - lt_rows) * (tile_t - tile_s), 0.0), axis=-1
        )
        return (grad_acc, kl_acc)

    grad_acc, kl_acc = lax.fori_loop(0, steps, second_one_block, start_grads)
    kl_rows = kl_acc - own_lse[:, 0] + own_lse[:, 1]
    kl_part = jnp.sum(jnp.where(own_live, kl_rows, 0.0))
    count_part = jnp.sum(own_live.astype(jnp.float32))
    kl_total, count_total = lax.psum((kl_part, count_part), ("head", "seq"))
    loss = (kl_total / (count_total / n_head * 2.0 * REL_HEADS)).reshape(1)
    grad_query = jnp.transpose(grad_acc[0], (1, 0, 2)).reshape(1, rows, half_width)
    grad_value = jnp.transpose(grad_acc[1], (1, 0, 2)).reshape(1, rows, half_width)
    return (grad_query, grad_value, loss)


def solution(mesh):
    return jax.shard_map(
        shards,
        mesh=mesh,
        in_specs=(
            P("doc", "seq"),
            P("doc", "seq", "head"),
            P("doc", "seq", "head"),
            P("doc", "seq", None),
            P("doc", "seq", None),
            P(),
            P(),
        ),
        out_specs=(P("doc", "seq", "head"), P("doc", "seq", "head"), P("doc")),
        check_vma=False,
    )
```

profile of v0, /device:TPU:0, one launch (start us, length us, event | category | flops | bytes accessed | tf_op | source)
XLA Modules:
  0.0 1144.3 jit_solution(16924662519127804386)
XLA Ops:
  34.6 9.1 reduce-scatter.2.cloned.1.call-done
  45.6 95.5 %all-gather = s32[1,16384]{1,0:T(1,128)S(1)} all-gather(s32[1,512]{1,0:T(1,128)S(1)} %copy-done.1), channel_id=2, replica_groups=mesh['doc'=2,'head'=2,'seq'=32] {'seq'}, dimensions={1}, use_global_device_ids=true | all-gather | bytes 67584 | tf_op jit(solution)/shard_map/all_gather | solution.py:99
  141.8 55.2 %all-gather.3.cloned.1.call-done = bf16[16384,4,128]{0,2,1:T(8,128)(2,1)} async-done(((bf16[512,4,128]{0,2,1:T(8,128)(2,1)}), bf16[16384,4,128]{0,2,1:T(8,128)(2,1)}) %all-gather.3.cloned.1.call-update) | async-done | bytes 16777232 | tf_op jit(solution)/shard_map/all_gather | solution.py:98
  197.0 287.9 %while.32 = (s32[]{:T(128)}, f32[2,2,2,512]{3,2,1,0:T(2,128)S(1)}, f32[2,2,2,512]{3,2,1,0:T(2,128)S(1)}, s32[16384]{0:T(1024)S(1)}, bf16[16384,4,128]{0,2,1:T(8,...) while((s32[]{:T(128)}, f32[2,2,2,512]{3,2,1,0:T(2,128)S(1)}, ...), condition=%wide.region_4.5_spmd.clone, body=%wide.region_1.4_spmd.clone.sunk | while | flops 566252544 | bytes 37444772 | solution.py:110
  198.3 8.8 select_reduce_fusion.6
  216.3 8.8 select_reduce_fusion.6
  252.3 8.8 select_reduce_fusion.6
  270.3 8.8 select_reduce_fusion.6
  288.3 8.8 select_reduce_fusion.6
  324.3 8.8 select_reduce_fusion.6
  342.3 8.8 select_reduce_fusion.6
  360.3 8.8 select_reduce_fusion.6
  414.3 8.8 select_reduce_fusion.6
  485.0 93.4 %all_gather.11 = f32[16384,2,2,2]{0,3,1,2:T(2,128)S(1)} all-gather(f32[512,2,2,2]{0,3,1,2:T(2,128)S(1)} %bitcast.149), channel_id=1, replica_groups=mesh['doc'=2,'head'=2,'seq'=32] {'seq'}, dimensions={0}, use_global_device_ids=true | all-gather | bytes 540672 | tf_op jit(solution)/shard_map/all_gather | solution.py:112
  578.4 381.6 %while.33 = (s32[]{:T(128)}, f32[2,2,512,64]{2,3,1,0:T(8,128)S(1)}, f32[2,2,512]{2,1,0:T(2,128)S(1)}, pred[512]{0:T(512)(128)(4,1)S(1)}, s32[16384]{0:T(1024)S(1...) while((s32[]{:T(128)}, f32[2,2,512,64]{2,3,1,0:T(8,128)S(1)}, ...), condition=%wide.region_7.8_spmd.clone, body=%wide.region_5.7_spmd.clone.sunk | while | flops 841878528 | bytes 124484320 | solution.py:160
  579.7 9.1 multiply_bitcast_fusion.2
  589.2 9.6 fusion.28
  603.5 9.1 multiply_bitcast_fusion.2
  613.0 9.6 fusion.28
  627.4 9.1 multiply_bitcast_fusion.2
  636.9 9.6 fusion.28
  651.2 9.1 multiply_bitcast_fusion.2
  660.7 9.6 fusion.28
  675.1 9.1 multiply_bitcast_fusion.2
  684.6 9.6 fusion.28
  698.9 9.1 multiply_bitcast_fusion.2
  708.4 9.6 fusion.28
  722.8 9.1 multiply_bitcast_fusion.2
  732.3 9.6 fusion.28
  746.6 9.1 multiply_bitcast_fusion.2
  756.1 9.6 fusion.28
  770.5 9.1 multiply_bitcast_fusion.2
  780.0 9.6 fusion.28
  794.3 9.1 multiply_bitcast_fusion.2
  803.8 9.6 fusion.28
  818.2 9.1 multiply_bitcast_fusion.2
  827.7 9.6 fusion.28
  842.0 9.1 multiply_bitcast_fusion.2
  851.5 9.6 fusion.28
  865.9 9.1 multiply_bitcast_fusion.2
  875.4 9.6 fusion.28
  889.7 9.1 multiply_bitcast_fusion.2
  899.2 9.6 fusion.28
  913.6 9.1 multiply_bitcast_fusion.2
  923.1 9.6 fusion.28
  937.4 9.1 multiply_bitcast_fusion.2
  946.9 9.6 fusion.28
  962.3 172.7 %all-reduce = (f32[]{:T(128)}, f32[]{:T(128)}) all-reduce(f32[]{:T(128)} %fusion.7, f32[]{:T(128)} %convert_reduce_fusion), channel_id=1, replica_groups=mesh['doc'=2,'head'=2,'seq'=32] {'head','seq'}, use_global_device_ids=true, to_apply=%region_9.10 | all-reduce | flops 2 | bytes 16 | tf_op jit(solution)/shard_map/psum | solution.py:164
  (293 shorter events, 303.7 us)
Async XLA Ops:
  7.2 38.4 %copy-start.1 = (s32[1,512]{1,0:T(1,128)S(1)}, s32[1,512]{1,0:T(1,128)}, u32[]{:S(2)}) copy-start(s32[1,512]{1,0:T(1,128)} %param.11) | copy-start | bytes 6148
  7.2 36.5 %reduce-scatter.2.cloned.1.call-start = ((), (), s32[]{:S(2)}) async-start(), calls=%async_computation.1 | async-start | bytes 786432 | tf_op jit(solution)/shard_map/reduce_scatter | solution.py:51
  23.9 173.1 %all-gather.3.cloned.1.call-start = ((), (), s32[]{:S(2)}) async-start(), calls=%async_computation.2 | async-start | bytes 17301504 | tf_op jit(solution)/shard_map/all_gather | solution.py:98
  589.2 10.7 copy-start
  613.0 10.7 copy-start
  636.9 10.7 copy-start
  660.7 10.7 copy-start
  684.6 10.7 copy-start
  708.4 10.7 copy-start
  732.3 10.7 copy-start
  756.1 10.7 copy-start
  780.0 10.7 copy-start
  803.8 10.7 copy-start
  827.7 10.7 copy-start
  851.5 10.7 copy-start
  875.4 10.7 copy-start
  899.2 10.7 copy-start
  923.1 10.7 copy-start
  946.9 10.7 copy-start
Sparse Core Ops, SparseCore 0:
  24.0 19.5 reduce-scatter.1
  46.8 150.1 all-gather.2
where the time goes:
time: 1150 us; the launch traced here: 1140 us
  matrix products  440 us (38%)
  blocking collectives  362 us (31%)
  other arithmetic  172 us (15%)
  local copies, waits for them, and re-layouts  70.8 us (6%)
  waiting for transfers between devices  64.3 us (6%)
  between operations  34.1 us (3%)
    dot_general x32, matrix products, score_tiles(): jnp.einsum('ikshd,jkshd->kshij', own_five, key_five, preferred_element_ty...  286 us
    psum x1, blocking collectives, shards(): kl_total, count_total = lax.psum((kl_part, count_part), ('head', 'seq'))  173 us
    dot_general x16, matrix products, second_one_block(): jnp.einsum('khij,jkhd->khid', weights, sub[:, :, 1], preferred_element_ty...  154 us
    reduce_sum x16, other arithmetic, row_update(): jnp.sum(jnp.where(alive, jnp.exp(tiles - new_max[..., None]), 0.0), axis=-1)  125 us
    all_gather x1, blocking collectives, shards(): lax.all_gather(own_ids, 'seq', axis=0, tiled=True)  95.5 us
    all_gather x1, blocking collectives, shards(): lax.all_gather(jnp.transpose(own_lse, (3, 0, 1, 2)), 'seq', axis=0, tiled...  93.4 us
    all_gather x1, waiting for transfers between devices, shards(): lax.all_gather(features, 'seq', axis=0, tiled=True)  55.2 us
    reduce_sum x16, other arithmetic, second_one_block(): jnp.sum(jnp.where(both, jnp.exp(tile_t - lt_rows) * (tile_t - tile_s), 0....  37.1 us
  transfers between devices with their start and end apart: 2, of which 2 were waited for; matrix products, arithmetic and copies ran while one was open for 0% of the time, Pallas kernels for 0%

commit v1 on v0

v1 whole, which is shorter than its diff:
```python
import functools

import jax
import jax.numpy as jnp
from jax import lax
from jax.experimental import pallas as pl
from jax.experimental.pallas import tpu as pltpu
from jax.sharding import PartitionSpec as P

HEAD_DIM = 128
W = 64
PER_HEAD = HEAD_DIM // W
T_GROUP = 8
S_GROUP = 7
REL_HEADS = 4
LEN = 16384
ROWS = 512
PIECE = ROWS + 16
OWN = 2048
TOP_BOUND = 162.0
LN2 = 0.6931471805599453
SHIFT = 74.0
FAST_TOP = 130.0
BJ = 1024
F32 = jnp.float32
BF16 = jnp.bfloat16
MESH = pl.DeviceIdType.MESH
VMEM = pltpu.VMEM
ANY = pl.ANY


def coords():
    doc = lax.axis_index("doc")
    head = lax.axis_index("head")
    seq = lax.axis_index("seq")
    return doc, head, seq // 8, (seq // 2) % 4, seq % 2


def device(doc, head, x, z, yh):
    return (doc, head, (x * 4 + z) * 2 + yh)


def same(a, b):
    return (a[0] == b[0]) & (a[1] == b[1]) & (a[2] == b[2])


def params(**kw):
    return pltpu.CompilerParams(vmem_limit_bytes=56 * 2**20, **kw)


def pick_kernel(tp, sp, ids, tq, tv, sq, sv, msg_a, msg_b, tw, sw, sem):
    head = lax.axis_index("head")
    copies = []

    def fetch(src, block, dst):
        start = pl.multiple_of((block // 2) * 128, 128)
        copy = pltpu.make_async_copy(src.at[:, pl.ds(start, 128)], dst, sem.at[len(copies)])
        copy.start()
        copies.append(copy)

    q_blocks = tq.shape[1] // W
    v_blocks = tv.shape[1] // W
    for r in range(REL_HEADS):
        b = tp[r]
        vb = (b // PER_HEAD) // T_GROUP * PER_HEAD + b % PER_HEAD
        fetch(tq, b % q_blocks, tw.at[0, r])
        fetch(tv, vb % v_blocks, tw.at[1, r])
    for e in range(2):
        b = sp[head * 2 + e]
        vb = (b // PER_HEAD) // S_GROUP * PER_HEAD + b % PER_HEAD
        fetch(sq, b, sw.at[0, e])
        fetch(sv, vb, sw.at[1, e])
    for copy in copies:
        copy.wait()

    def half(w, b):
        return jnp.where(b % 2 == 0, w[:, :W], w[:, W:])

    live = (ids[...] != 0).astype(F32)
    tail = jnp.concatenate([live, jnp.zeros((12, 128), F32)], axis=0).astype(BF16)
    for k in range(2):
        for e in range(2):
            r = head * 2 + e
            t = half(tw[k, r], tp[r])
            s = half(sw[k, e], sp[r])
            msg_a[k, e, 0:ROWS, :] = jnp.concatenate([t, s], axis=1)
            msg_a[k, e, ROWS:PIECE, :] = tail
            r = (1 - head) * 2 + e
            t = half(tw[k, r], tp[r])
            msg_b[k, e] = jnp.concatenate([t[: ROWS // 2], t[ROWS // 2 :]], axis=1)


def pick(tp, sp, ids, tq, tv, sq, sv):
    smem = pl.BlockSpec(memory_space=pltpu.SMEM)
    vmem = pl.BlockSpec(memory_space=VMEM)
    hbm = pl.BlockSpec(memory_space=ANY)
    return pl.pallas_call(
        pick_kernel,
        out_shape=(
            jax.ShapeDtypeStruct((2, 2, PIECE, 128), BF16),
            jax.ShapeDtypeStruct((2, 2, ROWS // 2, 128), BF16),
        ),
        in_specs=[smem, smem, vmem, hbm, hbm, hbm, hbm],
        out_specs=(vmem, vmem),
        scratch_shapes=[
            VMEM((2, 4, ROWS, 128), BF16),
            VMEM((2, 2, ROWS, 128), BF16),
            pltpu.SemaphoreType.DMA((12,)),
        ],
        compiler_params=params(),
    )(tp, sp, ids, tq, tv, sq, sv)


def greet(peers, me):
    barrier = pltpu.get_barrier_semaphore()
    count = 0
    for peer in peers:
        other = jnp.logical_not(same(peer, me))

        @pl.when(other)
        def _():
            pl.semaphore_signal(barrier, inc=1, device_id=peer, device_id_type=MESH)

        count = count + other.astype(jnp.int32)
    pl.semaphore_wait(barrier, count)


def gather_kernel(
    tp, msg_a, msg_b, out, got_a, got_b, chunk,
    sa, sb, ra, rb, s_own, s_core, s_up, s_dn, r_core, r_up, r_dn,
):
    doc, head, x, z, yh = coords()
    me = device(doc, head, x, z, yh)
    core = device(1 - doc, head, x, z, yh)
    up = device(doc, head, x, (z + 1) % 4, yh)
    down = device(doc, head, x, (z + 3) % 4, yh)
    to_a = [[device(yh, head, 2 * doc + k, z, e) for e in range(2)] for k in range(2)]
    to_b = [[device(yh, 1 - head, 2 * doc + k, z, e) for e in range(2)] for k in range(2)]
    from_doc = x // 2
    sources = [device(from_doc, h, xs, z, doc) for h in range(2) for xs in range(4)]
    greet(to_a[0] + to_a[1] + to_b[0] + to_b[1] + sources + [core, up, down], me)

    for k in range(2):
        for e in range(2):
            mine = same(to_a[k][e], me)

            @pl.when(mine)
            def _():
                pltpu.make_async_copy(msg_a.at[k, e], got_a.at[x], ra.at[x]).start()

            @pl.when(jnp.logical_not(mine))
            def _():
                pltpu.make_async_remote_copy(
                    msg_a.at[k, e], got_a.at[x], sa.at[k, e], ra.at[x],
                    device_id=to_a[k][e], device_id_type=MESH,
                ).start()

            pltpu.make_async_remote_copy(
                msg_b.at[k, e], got_b.at[x], sb.at[k, e], rb.at[x],
                device_id=to_b[k][e], device_id_type=MESH,
            ).start()

    own = tp[head * 2 + yh] // (REL_HEADS * 16) == head

    def remote(src, dst, send, recv, to):
        return pltpu.make_async_remote_copy(
            src, dst, send, recv, device_id=to, device_id_type=MESH
        )

    def place(i, zz, c):
        return out.at[i, zz, c]

    sends = []
    lane = lax.broadcasted_iota(jnp.int32, (ROWS // 2, 128), 1)
    for i in range(4):
        pltpu.make_async_copy(msg_a.at[0, 0], got_a.at[i], ra.at[i]).wait()
        pltpu.make_async_copy(msg_b.at[0, 0], got_b.at[i], rb.at[i]).wait()
        b = got_b[i]
        b_roll = jnp.concatenate([b[:, W:], b[:, :W]], axis=1)
        keep = jnp.logical_or(own, lane >= W)
        chunk[i, 0 : ROWS // 2] = jnp.where(keep, got_a[i, 0 : ROWS // 2], b)
        chunk[i, ROWS // 2 : ROWS] = jnp.where(keep, got_a[i, ROWS // 2 : ROWS], b_roll)
        chunk[i, ROWS:PIECE] = got_a[i, ROWS:PIECE]
        for copy in (
            remote(chunk.at[i], place(i, z, doc), s_up.at[i], r_dn.at[i], up),
            remote(chunk.at[i], place(i, z, doc), s_dn.at[i], r_up.at[i], down),
            remote(chunk.at[i], place(i, z, doc), s_core.at[i], r_core.at[i], core),
        ):
            copy.start()
            sends.append(copy)
        local = pltpu.make_async_copy(chunk.at[i], place(i, z, doc), s_own.at[i])
        local.start()
        sends.append(local)

    below, above, across = (z + 3) % 4, (z + 1) % 4, (z + 2) % 4

    def forward(src, send, recv, to):
        copy = remote(src, src, send, recv, to)
        copy.start()
        sends.append(copy)

    def arrived(ref, sem):
        pltpu.make_async_copy(ref, ref, sem).wait()

    for i in range(4):
        lo = place(i, below, doc)
        arrived(lo, r_dn.at[i])
        if i < 2:
            forward(lo, s_up.at[4 + i], r_dn.at[4 + i], up)
        forward(lo, s_core.at[4 + i], r_core.at[4 + i], core)
        hi = place(i, above, doc)
        arrived(hi, r_up.at[i])
        if i >= 2:
            forward(hi, s_dn.at[2 + i], r_up.at[2 + i], down)
        forward(hi, s_core.at[8 + i], r_core.at[8 + i], core)
    for i in range(4):
        far = place(i, across, doc)
        arrived(far, r_dn.at[4 + i] if i < 2 else r_up.at[2 + i])
        forward(far, s_core.at[12 + i], r_core.at[12 + i], core)
    for i in range(4):
        arrived(place(i, z, 1 - doc), r_core.at[i])
        arrived(place(i, below, 1 - doc), r_core.at[4 + i])
        arrived(place(i, above, 1 - doc), r_core.at[8 + i])
        arrived(place(i, across, 1 - doc), r_core.at[12 + i])
    for copy in sends:
        if hasattr(copy, "wait_send") and copy.is_remote:
            copy.wait_send()
        else:
            copy.wait()
    for k in range(2):
        for e in range(2):

            @pl.when(jnp.logical_not(same(to_a[k][e], me)))
            def _():
                remote(msg_a.at[k, e], got_a.at[x], sa.at[k, e], ra.at[x], to_a[k][e]).wait_send()

            remote(msg_b.at[k, e], got_b.at[x], sb.at[k, e], rb.at[x], to_b[k][e]).wait_send()


def gather(tp, msg_a, msg_b):
    dma = pltpu.SemaphoreType.DMA
    vmem = pl.BlockSpec(memory_space=VMEM)
    return pl.pallas_call(
        gather_kernel,
        out_shape=jax.ShapeDtypeStruct((4, 4, 2, PIECE, 128), BF16),
        in_specs=[pl.BlockSpec(memory_space=pltpu.SMEM), vmem, vmem],
        out_specs=pl.BlockSpec(memory_space=ANY),
        scratch_shapes=[
            VMEM((4, PIECE, 128), BF16),
            VMEM((4, ROWS // 2, 128), BF16),
            VMEM((4, PIECE, 128), BF16),
            dma((2, 2)), dma((2, 2)), dma((4,)), dma((4,)),
            dma((4,)), dma((16,)), dma((6,)), dma((6,)), dma((16,)), dma((6,)), dma((6,)),
        ],
        compiler_params=params(collective_id=0, has_side_effects=True),
    )(tp, msg_a, msg_b)


def live_count(feats):
    total = jnp.zeros((16, 128), F32)
    for i in range(4):
        for zz in range(4):
            for c in range(2):
                total = total + feats[i, zz, c, ROWS:PIECE, :].astype(F32)
    return jnp.sum(total).astype(jnp.int32)


def fill_columns(feats, n, xa, ya):
    lane = lax.broadcasted_iota(jnp.int32, (ROWS, 128), 1)
    row = lax.broadcasted_iota(jnp.int32, (ROWS, 128), 0)
    ones = jnp.where((lane >= W) & (lane < W + 3), 1.0, 0.0)

    def one(b, _):
        f = feats[b // 8, (b // 2) % 4, b % 2, 0:ROWS, :]
        rest = jnp.where((lane == W + 3) & (row + b * ROWS >= n), -30000.0, ones).astype(BF16)
        at = pl.ds(pl.multiple_of(b * ROWS, ROWS), ROWS)
        xa[at, :] = jnp.where(lane < W, f, rest)
        turned = jnp.concatenate([f[:, W:], f[:, :W]], axis=1)
        ya[at, :] = jnp.where(lane < W, turned, rest)
        return 0

    lax.fori_loop(0, (n + ROWS - 1) // ROWS, one, 0)
    b = jnp.minimum((n + ROWS - 1) // ROWS, LEN // ROWS - 1)

    @pl.when(b * ROWS >= n)
    def _():
        one(b, 0)


def own_rows(feats, d, own):
    for m in range(16):
        b = 2 * m + d // 4
        part = feats[b // 8, (b // 2) % 4, b % 2, pl.ds(pl.multiple_of((d % 4) * 128, 128), 128), :]
        own[:, m * 128 : (m + 1) * 128] = part.T


def self_scores(feat):
    f = feat.astype(F32)
    return jnp.sum(f * f, axis=0, keepdims=True) * 0.125


def row_shift(own_score):
    room = 75.0 - (jnp.sqrt(own_score * TOP_BOUND) - own_score)
    k = jnp.floor(jnp.maximum(jnp.minimum(room, own_score), 0.0) * (1.0 / LN2))
    return own_score - k * LN2, k


def fill_rows(own, xi, yi):
    for ref, lo in ((xi, 0), (yi, W)):
        feat = own[lo : lo + W, :]
        shift, _ = row_shift(self_scores(feat))
        one = shift.astype(BF16).astype(F32)
        two = (shift - one).astype(BF16).astype(F32)
        three = shift - one - two
        at = lax.broadcasted_iota(jnp.int32, (16, OWN), 0)
        rest = jnp.where(at == 0, -one, jnp.where(at == 1, -two, jnp.where(at == 2, -three, jnp.where(at == 3, 1.0, 0.0))))
        ref[0:W, :] = feat * jnp.asarray(0.125, BF16)
        ref[W : W + 16, :] = rest.astype(BF16)
        ref[W + 16 :, :] = jnp.zeros((128 - W - 16, OWN), BF16)


def own_live(n, d):
    lane = lax.broadcasted_iota(jnp.int32, (1, OWN), 1)
    token = ((lane // 128) * 8 + d) * 128 + lane % 128
    return token < n


def row_tiles(n, d, tile):
    blocks = jnp.clip((n - d * 128 + 1023) // 1024, 0, 16)
    quarters = (blocks + 1) // 2
    full = quarters // 4

    def big(b, _):
        tile(pl.multiple_of(b * 1024, 1024), 1024)
        return 0

    lax.fori_loop(0, full, big, 0)
    rest = quarters % 4

    @pl.when(rest == 3)
    def _():
        tile(pl.multiple_of(full * 1024, 1024), 1024)

    @pl.when(rest == 2)
    def _():
        tile(pl.multiple_of(full * 1024, 1024), 512)

    @pl.when(rest == 1)
    def _():
        tile(pl.multiple_of(full * 1024, 1024), 256)


def sums_kernel(feats, out, own, xa, ya, xi, yi, sums):
    doc, _, _, z, _ = coords()
    d = z * 2 + doc
    n = live_count(feats)
    fill_columns(feats, n, xa, ya)
    own_rows(feats, d, own)
    fill_rows(own, xi, yi)
    sums[...] = jnp.ones_like(sums)
    steps = (n + BJ - 1) // BJ

    def tile(start, width):
        at = pl.ds(start, width)

        def step(j, carry):
            js = pl.ds(pl.multiple_of(j * BJ, BJ), BJ)
            t = jnp.exp(jnp.dot(xa[js, :], xi[:, at], preferred_element_type=F32))
            s = jnp.exp(jnp.dot(ya[js, :], yi[:, at], preferred_element_type=F32))
            add_t = jnp.sum(t.reshape(BJ // 8, 8, width), axis=0)
            add_s = jnp.sum(s.reshape(BJ // 8, 8, width), axis=0)
            return carry[0] + add_t, carry[1] + add_s

        zero = jnp.zeros((8, width), F32)
        t, s = lax.fori_loop(0, steps, step, (zero, zero))
        sums[0:1, at] = jnp.sum(t, axis=0, keepdims=True)
        sums[1:2, at] = jnp.sum(s, axis=0, keepdims=True)

    row_tiles(n, d, tile)
    live = own_live(n, d)
    st = self_scores(own[0:W, :])
    ss = self_scores(own[W:, :])
    lt = row_shift(st)[0] + jnp.log(sums[0:1, :])
    ls = row_shift(ss)[0] + jnp.log(sums[1:2, :])
    top = jnp.max(jnp.where(live, jnp.maximum(st, ss), 0.0))
    out[0:1, :] = jnp.where(live, lt, 0.0)
    out[1:2, :] = jnp.where(live, ls, 0.0)
    out[2:3, :] = jnp.full((1, OWN), top)
    out[3:4, :] = jnp.full((1, OWN), n.astype(F32))
    out[4:8, :] = jnp.zeros((4, OWN), F32)


def sums(feats):
    return pl.pallas_call(
        sums_kernel,
        out_shape=jax.ShapeDtypeStruct((8, OWN), F32),
        in_specs=[pl.BlockSpec(memory_space=VMEM)],
        out_specs=pl.BlockSpec(memory_space=VMEM),
        scratch_shapes=[
            VMEM((128, OWN), BF16),
            VMEM((LEN, 128), BF16),
            VMEM((LEN, 128), BF16),
            VMEM((128, OWN), BF16),
            VMEM((128, OWN), BF16),
            VMEM((8, OWN), F32),
        ],
        compiler_params=params(),
    )(feats)


def share_kernel(mine, out, s_own, send, recv):
    doc, head, x, z, yh = coords()
    me = device(doc, head, x, z, yh)
    d = z * 2 + doc
    peers = []
    for step in range(1, 8):
        p = (d + step) % 8
        peers.append(device(p % 2, head, x, p // 2, yh))
    greet(peers, me)
    copies = []
    for step in range(1, 8):
        copy = pltpu.make_async_remote_copy(
            mine, out.at[d], send.at[step - 1], recv.at[step - 1],
            device_id=peers[step - 1], device_id_type=MESH,
        )
        copy.start()
        copies.append(copy)
    local = pltpu.make_async_copy(mine, out.at[d], s_own)
    local.start()
    for step in range(1, 8):
        p = (d + 8 - step) % 8
        pltpu.make_async_copy(mine, out.at[p], recv.at[step - 1]).wait()
    for copy in copies:
        copy.wait_send()
    local.wait()


def share(mine):
    dma = pltpu.SemaphoreType.DMA
    vmem = pl.BlockSpec(memory_space=VMEM)
    return pl.pallas_call(
        share_kernel,
        out_shape=jax.ShapeDtypeStruct((8, 8, OWN), F32),
        in_specs=[vmem],
        out_specs=vmem,
        scratch_shapes=[dma, dma((7,)), dma((7,))],
        compiler_params=params(collective_id=1, has_side_effects=True),
    )(mine)


def grads_kernel(feats, lse, grad, kl, own, xa, ya, xi, yi, vt, vs, ot, os_):
    doc, _, _, z, _ = coords()
    d = z * 2 + doc
    n = live_count(feats)
    fill_columns(feats, n, xa, ya)
    own_rows(feats, d, own)
    fill_rows(own, xi, yi)
    steps = (n + BJ - 1) // BJ

    def weigh(b, _):
        f = feats[b // 8, (b // 2) % 4, b % 2, 0:ROWS, :].T
        x, y = f[:W, :], f[W:, :]
        yf = y.astype(F32)
        at = pl.ds(pl.multiple_of(b * ROWS, ROWS), ROWS)
        lt, ls = [], []
        for q in range(4):
            m = (b * 4 + q) // 8
            dd = (b * 4 + q) % 8
            ms = pl.ds(pl.multiple_of(m * 128, 128), 128)
            lt.append(lse[dd, 0:1, ms])
            ls.append(lse[dd, 1:2, ms])
        lane = lax.broadcasted_iota(jnp.int32, (1, ROWS), 1) + b * ROWS
        wt = jnp.where(lane < n, jnp.exp(SHIFT - jnp.concatenate(lt, axis=1)), 0.0)
        ws = jnp.where(lane < n, jnp.exp(SHIFT - jnp.concatenate(ls, axis=1)), 0.0)
        vt[0:W, at] = y
        vt[W : 2 * W, at] = (yf * wt).astype(BF16)
        vt[2 * W :, at] = x
        vs[0:W, at] = y
        vs[W:, at] = (yf * ws).astype(BF16)
        return 0

    lax.fori_loop(0, steps * (BJ // ROWS), weigh, 0)
    ot[...] = jnp.zeros_like(ot)
    os_[...] = jnp.zeros_like(os_)

    def tile(start, width):
        at = pl.ds(start, width)

        def step(j, _):
            js = pl.ds(pl.multiple_of(j * BJ, BJ), BJ)
            t = jnp.exp(jnp.dot(xa[js, :], xi[:, at], preferred_element_type=F32)).astype(BF16)
            s = jnp.exp(jnp.dot(ya[js, :], yi[:, at], preferred_element_type=F32)).astype(BF16)
            ot[:, at] += jnp.dot(vt[:, js], t, preferred_element_type=F32)
            os_[:, at] += jnp.dot(vs[:, js], s, preferred_element_type=F32)
            return 0

        lax.fori_loop(0, steps, step, 0)

    row_tiles(n, d, tile)
    live = own_live(n, d)
    x = own[0:W, :].astype(F32)
    y = own[W:, :].astype(F32)
    lt = lse[d, 0:1, :]
    ls = lse[d, 1:2, :]

    def finish(acc, feat, l):
        shift, k = row_shift(self_scores(feat))
        by_row = jnp.exp(shift - l)
        by_col = jnp.exp((shift - SHIFT) * 0.5)
        exact = y * jnp.exp(SHIFT - l)
        missing = (exact - exact.astype(BF16).astype(F32)) * jnp.exp2(k)
        return acc[0:W, :] * by_row + (acc[W : 2 * W, :] + missing) * by_col * by_col, by_row

    gs, _ = finish(os_, own[W:, :], ls)
    gt, by_row = finish(ot, own[0:W, :], lt)
    grad[...] = jnp.where(live, (gs - gt) * 0.125, 0.0)
    moved = jnp.sum(x * ot[2 * W :, :] - y * ot[0:W, :], axis=0, keepdims=True)
    rows = jnp.where(live, moved * by_row * 0.125 - lt + ls, 0.0)
    acc = rows[:, 0:128]
    for m in range(1, 16):
        acc = acc + rows[:, m * 128 : (m + 1) * 128]
    at = lax.broadcasted_iota(jnp.int32, (8, 128), 0)
    kl[...] = jnp.where(at == 0, acc, jnp.where(at == 1, n.astype(F32), 0.0))


def grads(feats, lse):
    vmem = pl.BlockSpec(memory_space=VMEM)
    return pl.pallas_call(
        grads_kernel,
        out_shape=(jax.ShapeDtypeStruct((W, OWN), F32), jax.ShapeDtypeStruct((8, 128), F32)),
        in_specs=[vmem, vmem],
        out_specs=(vmem, vmem),
        scratch_shapes=[
            VMEM((128, OWN), BF16),
            VMEM((LEN, 128), BF16),
            VMEM((LEN, 128), BF16),
            VMEM((128, OWN), BF16),
            VMEM((128, OWN), BF16),
            VMEM((3 * W, LEN), BF16),
            VMEM((2 * W, LEN), BF16),
            VMEM((3 * W, OWN), F32),
            VMEM((2 * W, OWN), F32),
        ],
        compiler_params=params(),
    )(feats, lse)


def grads_wide(feats, lse):
    doc, _, _, z, _ = coords()
    d = z * 2 + doc
    n = lse[0, 3, 0].astype(jnp.int32)
    f = feats[:, :, :, :ROWS, :].reshape(LEN // 1024, 8, 128, 128)
    mine = lax.dynamic_index_in_dim(f, d, 1, keepdims=False).reshape(OWN, 128)
    cols = f.reshape(LEN // 1024, 1024, 128)
    col_lse = jnp.transpose(lse[:, :2].reshape(8, 2, 16, 128), (2, 1, 0, 3)).reshape(16, 2, 1024)
    own_lse = lax.dynamic_index_in_dim(lse, d, 0, keepdims=False)
    lt, ls = own_lse[0][:, None], own_lse[1][:, None]
    lane = jnp.arange(OWN)
    live = (((lane // 128) * 8 + d) * 128 + lane % 128 < n)[:, None]

    def step(j, carry):
        grad, kl = carry
        c = lax.dynamic_index_in_dim(cols, j, 0, keepdims=False)
        cl = lax.dynamic_index_in_dim(col_lse, j, 0, keepdims=False)
        both = live & (j * 1024 + jnp.arange(1024) < n)[None, :]
        t = jnp.dot(mine[:, :W], c[:, :W].T, preferred_element_type=F32) * 0.125
        s = jnp.dot(mine[:, W:], c[:, W:].T, preferred_element_type=F32) * 0.125
        pt = jnp.where(both, jnp.exp(t - lt), 0.0)
        rows = jnp.where(both, jnp.exp(s - ls), 0.0) - pt
        columns = jnp.where(both, jnp.exp(s - cl[1:2]) - jnp.exp(t - cl[0:1]), 0.0)
        w = (rows + columns).astype(BF16)
        grad = grad + jnp.dot(w, c[:, W:], preferred_element_type=F32) * 0.125
        return grad, kl + jnp.sum(pt * (t - s), axis=1, keepdims=True)

    zero = (jnp.zeros((OWN, W), F32), jnp.zeros((OWN, 1), F32))
    grad, kl = lax.fori_loop(0, 16, step, zero)
    rows = jnp.where(live, kl - lt + ls, 0.0).reshape(16, 128)
    tile = jnp.concatenate(
        [jnp.sum(rows, axis=0, keepdims=True), jnp.full((1, 128), n.astype(F32)), jnp.zeros((6, 128), F32)]
    )
    return grad.T, tile


def give_kernel(grad, kl, gq, gv, loss, got, got_kl, sums, got_sum, sg, rg, sk, rk, ss, rs):
    doc, head, x, z, yh = coords()
    me = device(doc, head, x, z, yh)
    d = z * 2 + doc
    to = [device(x // 2, head, m // 4, m % 4, z // 2) for m in range(16)]
    sources = []
    for k in range(2):
        for e in range(2):
            for q in range(4):
                sources.append(device(q % 2, head, 2 * doc + k, 2 * yh + q // 2, e))
    ring = [device(doc, 1 - head, x, z, yh), device(doc, head, x, z, 1 - yh), device(doc, 1 - head, x, z, 1 - yh)]
    greet(to + sources + ring, me)
    kind, part, q = x % 2, yh, d % 4
    slot = (kind * 2 + part) * 4 + q
    where = pl.ds(pl.multiple_of(part * W, W), W)
    for m in range(16):
        mine = same(to[m], me)
        src = grad.at[:, m * 128 : (m + 1) * 128]

        @pl.when(mine)
        def _():
            pltpu.make_async_copy(src, got.at[kind, q, where], rg.at[slot]).start()
            pltpu.make_async_copy(kl, got_kl.at[slot], rk.at[slot]).start()

        @pl.when(jnp.logical_not(mine))
        def _():
            pltpu.make_async_remote_copy(
                src, got.at[kind, q, where], sg.at[m], rg.at[slot], device_id=to[m], device_id_type=MESH
            ).start()
            pltpu.make_async_remote_copy(
                kl, got_kl.at[slot], sk.at[m], rk.at[slot], device_id=to[m], device_id_type=MESH
            ).start()

    total = jnp.zeros((8, 128), F32)
    for i in range(16):
        pltpu.make_async_copy(kl, got_kl.at[i], rk.at[i]).wait()
        total = total + got_kl[i]
    sums[...] = total
    swaps = []
    for i in range(3):
        copy = pltpu.make_async_remote_copy(
            sums, got_sum.at[i], ss.at[i], rs.at[i], device_id=ring[i], device_id_type=MESH
        )
        copy.start()
        swaps.append(copy)
    for k, out in ((0, gq), (1, gv)):
        for q_ in range(4):
            for e in range(2):
                part_ref = got.at[k, q_, pl.ds(e * W, W)]
                pltpu.make_async_copy(part_ref, part_ref, rg.at[(k * 2 + e) * 4 + q_]).wait()
            out[q_ * 128 : (q_ + 1) * 128, :] = got[k, q_].T
    for i in range(3):
        swaps[i].wait_recv()
        total = total + got_sum[i]
    for i in range(3):
        swaps[i].wait_send()
    kl_sum = jnp.sum(total[0:1, :], axis=1, keepdims=True)
    count = total[1:2, 0:1] * (1.0 / 64.0)
    loss[...] = jnp.broadcast_to(kl_sum / (count * (2.0 * REL_HEADS)), (8, 128))
    for m in range(16):
        src = grad.at[:, m * 128 : (m + 1) * 128]

        @pl.when(jnp.logical_not(same(to[m], me)))
        def _():
            pltpu.make_async_remote_copy(
                src, got.at[kind, q, where], sg.at[m], rg.at[slot], device_id=to[m], device_id_type=MESH
            ).wait_send()
            pltpu.make_async_remote_copy(
                kl, got_kl.at[slot], sk.at[m], rk.at[slot], device_id=to[m], device_id_type=MESH
            ).wait_send()


def give(grad, kl):
    dma = pltpu.SemaphoreType.DMA
    vmem = pl.BlockSpec(memory_space=VMEM)
    out = jax.ShapeDtypeStruct((ROWS, 128), F32)
    return pl.pallas_call(
        give_kernel,
        out_shape=(out, out, jax.ShapeDtypeStruct((8, 128), F32)),
        in_specs=[vmem, vmem],
        out_specs=(vmem, vmem, vmem),
        scratch_shapes=[
            VMEM((2, 4, 128, 128), F32),
            VMEM((16, 8, 128), F32),
            VMEM((8, 128), F32),
            VMEM((3, 8, 128), F32),
            dma((16,)), dma((16,)), dma((16,)), dma((16,)), dma((3,)), dma((3,)),
        ],
        compiler_params=params(collective_id=2, has_side_effects=True),
    )(grad, kl)


def shards(token_ids, teacher_query, teacher_value, student_query, student_value, teacher_pick, student_pick):
    msg_a, msg_b = pick(
        teacher_pick, student_pick, token_ids.reshape(4, 128),
        teacher_query[0], teacher_value[0], student_query[0], student_value[0],
    )
    feats = gather(teacher_pick, msg_a, msg_b)
    lse = share(sums(feats))
    fast = jnp.max(lse[:, 2, 0]) <= FAST_TOP
    grad, kl = lax.cond(fast, grads, grads_wide, feats, lse)
    gq, gv, loss = give(grad, kl)
    return gq[None], gv[None], loss[0, :1]


def solution(mesh):
    return jax.shard_map(
        shards,
        mesh=mesh,
        in_specs=(
            P("doc", "seq"),
            P("doc", "seq", "head"),
            P("doc", "seq", "head"),
            P("doc", "seq", None),
            P("doc", "seq", None),
            P(),
            P(),
        ),
        out_specs=(P("doc", "seq", "head"), P("doc", "seq", "head"), P("doc")),
        check_vma=False,
    )
```

time: 1150 us -> 213 us (0.19)
  matrix products: 440 us -> 0 us
  blocking collectives: 362 us -> 0 us
  Pallas kernels: 0 us -> 204 us
  other arithmetic: 172 us -> 0.61 us
  local copies, waits for them, and re-layouts: 70.8 us -> 6.49 us
  waiting for transfers between devices: 64.3 us -> 0 us
  between operations: 34.1 us -> 1.33 us
    dot_general x48 -> x0, matrix products: 440 us -> none  [the longest x32 286 us: score_tiles(): jnp.einsum('ikshd,jkshd->kshij', own_five, key_five, preferred_element_ty...]
    pallas_call x0 -> x6, Pallas kernels: none -> 204 us  [the longest x1 98.3 us: give(): pl.pallas_call(give_kernel, out_shape=(out, out, jax.ShapeDtypeStruct((8,...]
    all_gather x2 -> x0, blocking collectives: 189 us -> none  [the longest x1 95.5 us: shards(): lax.all_gather(own_ids, 'seq', axis=0, tiled=True)]
    psum x1 -> x0, blocking collectives: 173 us -> none  [shards(): kl_total, count_total = lax.psum((kl_part, count_part), ('head', 'seq'))]
    reduce_sum x34 -> x0, other arithmetic: 163 us -> none  [the longest x16 125 us: row_update(): jnp.sum(jnp.where(alive, jnp.exp(tiles - new_max[..., None]), 0.0), axis=-1)]
    all_gather x1 -> x0, waiting for transfers between devices: 55.2 us -> none  [shards(): lax.all_gather(features, 'seq', axis=0, tiled=True)]
    dynamic_slice x41 -> x0, local copies, waits for them, and re-layouts: 48.2 us -> none  [the longest x16 20.8 us: first_one_block(): lax.dynamic_slice_in_dim(whole_feats, step_idx * width, width, 0)]
    while x48 -> x0, local copies, waits for them, and re-layouts: 17.4 us -> none
  transfers between devices with their start and end apart: 2 -> 0, of which waited for: 2 -> 0; matrix products, arithmetic and copies ran while one was open for 0% -> 0% of each run, Pallas kernels for 0% -> 0%
where the time goes in v1:
time: 213 us
  Pallas kernels  204 us (96%)
  local copies, waits for them, and re-layouts  6.49 us (3%)
    pallas_call x1, Pallas kernels, give(): pl.pallas_call(give_kernel, out_shape=(out, out, jax.ShapeDtypeStruct((8,...  98.3 us
    pallas_call x1, Pallas kernels, gather(): pl.pallas_call(gather_kernel, out_shape=jax.ShapeDtypeStruct((4, 4, 2, PI...  35.8 us
    pallas_call x1, Pallas kernels, grads(): pl.pallas_call(grads_kernel, out_shape=(jax.ShapeDtypeStruct((W, OWN), F3...  34.1 us
    pallas_call x1, Pallas kernels, sums(): pl.pallas_call(sums_kernel, out_shape=jax.ShapeDtypeStruct((8, OWN), F32)...  21.1 us
    pallas_call x1, Pallas kernels, share(): pl.pallas_call(share_kernel, out_shape=jax.ShapeDtypeStruct((8, 8, OWN),...  10.3 us
    unnamed x4, local copies, waits for them, and re-layouts  5.3 us
    pallas_call x1, Pallas kernels, pick(): pl.pallas_call(pick_kernel, out_shape=(jax.ShapeDtypeStruct((2, 2, PIECE,...  4.54 us

profile of v1, /device:TPU:0, one launch (start us, length us, event | category | flops | bytes accessed | tf_op | source)
XLA Modules:
  0.0 212.8 jit_solution(8629782773868103769)
XLA Ops:
  0.6 4.5 %shard_map.94 = (bf16[2,2,528,128]{3,2,1,0:T(8,128)(2,1)}, bf16[2,2,256,128]{3,2,1,0:T(8,128)(2,1)}) custom-call(s32[4]{0:T(128)} %tp.3, s32[4]{0:T(128)} %sp.1, s32[4,128]{1,0:T(4,128)} %bitcast.104, bf16[512,4096]{1,0:T(8,128)(2,1)} %bitcast.88, bf16[512,512]{1,0:T(8,128)(2,1)} %bitcast.92, bf16[512,3584]{1,0:T(8,128)(2,1)} %bitcast.89, ...), custom_call_target="tpu_custom_call" | custom-call | tf_op jit(solution)/shard_map/pallas_call | solution.py:97
  5.2 35.8 %shard_map.95.feats = bf16[4,4,2,528,128]{4,3,2,1,0:T(8,128)(2,1)S(1)} custom-call(s32[4]{0:T(128)} %tp.3, bf16[2,2,528,128]{3,2,1,0:T(8,128)(2,1)} %get-tuple-element.192.msg_a, bf16[2,2,256,128]{3,2,1,0:T(8,128)(2,1)} %get-tuple-element.193.msg_b), custom_call_target="tpu_custom_call" | custom-call | tf_op jit(solution)/shard_map/pallas_call | solution.py:243
  41.0 0.0 copy-start
  41.0 2.0 copy-done
  43.0 21.1 %shard_map.96.mine = f32[8,2048]{1,0:T(8,128)} custom-call(bf16[4,4,2,528,128]{4,3,2,1,0:T(8,128)(2,1)S(1)} %shard_map.95.feats), custom_call_target="tpu_custom_call" | custom-call | tf_op jit(solution)/shard_map/pallas_call | solution.py:394
  64.1 10.3 %shard_map.97 = f32[8,8,2048]{2,1,0:T(8,128)S(1)} custom-call(f32[8,2048]{1,0:T(8,128)} %shard_map.96.mine), custom_call_target="tpu_custom_call" | custom-call | tf_op jit(solution)/shard_map/pallas_call | solution.py:441
  74.4 0.6 slice_reduce_fusion
  75.7 34.3 %conditional.1 = ((f32[64,2048]{1,0:T(8,128)S(1)}, f32[8,128]{1,0:T(8,128)S(1)})) conditional(s32[]{:T(128)} %convert_element_type.19, (bf16[4,4,2,528,128]{4,3,2,1,0:T(8,128)(2,1)}, f32[8,8,2048]{2,1,0:T(8,128)S(1)}) %tuple.65, (bf16[4,4,2,528,128]{4,3,2,1,0:T(8,128)(2,1)}, f32[8,8,2048]{2,1,0:T(8,128)S(1)}) %tuple.66), branch_computations={%region_1.6_spmd, %region_6.7_spmd} | conditional | flops 851920832 | bytes 72784856 | solution.py:684
  75.9 34.1 %branch_1_fun.1 = (f32[64,2048]{1,0:T(8,128)S(1)}, f32[8,128]{1,0:T(8,128)S(1)}) custom-call(bf16[4,4,2,528,128]{4,3,2,1,0:T(8,128)(2,1)} %get-tuple-element.180.feats, f32[8,8,2048]{2,1,0:T(8,128)S(1)} %get-tuple-element.181.lse), custom_call_target="tpu_custom_call" | custom-call | tf_op jit(solution)/shard_map/cond/branch_1_fun/pallas_call | solution.py:528
  110.0 98.3 %shard_map.98 = (f32[512,128]{1,0:T(8,128)}, f32[512,128]{1,0:T(8,128)}, f32[8,128]{1,0:T(8,128)}) custom-call(f32[64,2048]{1,0:T(8,128)S(1)} %get-tuple-element.194.grad, f32[8,128]{1,0:T(8,128)S(1)} %get-tuple-element.195.kl), custom_call_target="tpu_custom_call" | custom-call | tf_op jit(solution)/shard_map/pallas_call | solution.py:660
  208.3 1.2 slice.69
  209.5 1.7 copy.32
  211.1 1.7 copy.33
Async XLA Ops:
  41.0 2.0 copy-start

commit v2 on v1

--- a/solution.py
+++ b/solution.py
@@ -19,6 +19,7 @@
 OWN = 2048
 TOP_BOUND = 162.0
 LN2 = 0.6931471805599453
+LOG2E = 1.4426950408889634
 SHIFT = 74.0
 FAST_TOP = 130.0
 BJ = 1024
@@ -168,19 +169,20 @@
         )
 
     def place(i, zz, c):
-        return out.at[i, zz, c]
+        return out.at[order[i], zz, c]
 
     sends = []
     lane = lax.broadcasted_iota(jnp.int32, (ROWS // 2, 128), 1)
-    for i in range(4):
-        pltpu.make_async_copy(msg_a.at[0, 0], got_a.at[i], ra.at[i]).wait()
-        pltpu.make_async_copy(msg_b.at[0, 0], got_b.at[i], rb.at[i]).wait()
-        b = got_b[i]
+    order = [x, (x + 1) % 4, (x + 3) % 4, (x + 2) % 4]
+    for i, xs in enumerate(order):
+        pltpu.make_async_copy(msg_a.at[0, 0], got_a.at[xs], ra.at[xs]).wait()
+        pltpu.make_async_copy(msg_b.at[0, 0], got_b.at[xs], rb.at[xs]).wait()
+        b = got_b[xs]
         b_roll = jnp.concatenate([b[:, W:], b[:, :W]], axis=1)
         keep = jnp.logical_or(own, lane >= W)
-        chunk[i, 0 : ROWS // 2] = jnp.where(keep, got_a[i, 0 : ROWS // 2], b)
-        chunk[i, ROWS // 2 : ROWS] = jnp.where(keep, got_a[i, ROWS // 2 : ROWS], b_roll)
-        chunk[i, ROWS:PIECE] = got_a[i, ROWS:PIECE]
+        chunk[i, 0 : ROWS // 2] = jnp.where(keep, got_a[xs, 0 : ROWS // 2], b)
+        chunk[i, ROWS // 2 : ROWS] = jnp.where(keep, got_a[xs, ROWS // 2 : ROWS], b_roll)
+        chunk[i, ROWS:PIECE] = got_a[xs, ROWS:PIECE]
         for copy in (
             remote(chunk.at[i], place(i, z, doc), s_up.at[i], r_dn.at[i], up),
             remote(chunk.at[i], place(i, z, doc), s_dn.at[i], r_up.at[i], down),
@@ -265,26 +267,15 @@
     return jnp.sum(total).astype(jnp.int32)
 
 
-def fill_columns(feats, n, xa, ya):
-    lane = lax.broadcasted_iota(jnp.int32, (ROWS, 128), 1)
-    row = lax.broadcasted_iota(jnp.int32, (ROWS, 128), 0)
-    ones = jnp.where((lane >= W) & (lane < W + 3), 1.0, 0.0)
-
-    def one(b, _):
-        f = feats[b // 8, (b // 2) % 4, b % 2, 0:ROWS, :]
-        rest = jnp.where((lane == W + 3) & (row + b * ROWS >= n), -30000.0, ones).astype(BF16)
-        at = pl.ds(pl.multiple_of(b * ROWS, ROWS), ROWS)
-        xa[at, :] = jnp.where(lane < W, f, rest)
-        turned = jnp.concatenate([f[:, W:], f[:, :W]], axis=1)
-        ya[at, :] = jnp.where(lane < W, turned, rest)
-        return 0
-
-    lax.fori_loop(0, (n + ROWS - 1) // ROWS, one, 0)
-    b = jnp.minimum((n + ROWS - 1) // ROWS, LEN // ROWS - 1)
-
-    @pl.when(b * ROWS >= n)
-    def _():
-        one(b, 0)
+def block(feats, b):
+    return feats[b // 8, (b // 2) % 4, b % 2, 0:ROWS, :]
+
+
+def tile_scores(feats, j, rows):
+    parts = []
+    for half in range(BJ // ROWS):
+        parts.append(jnp.dot(block(feats, j * (BJ // ROWS) + half), rows, preferred_element_type=F32))
+    return jnp.concatenate(parts, axis=0)
 
 
 def own_rows(feats, d, own):
@@ -301,22 +292,18 @@
 
 def row_shift(own_score):
     room = 75.0 - (jnp.sqrt(own_score * TOP_BOUND) - own_score)
-    k = jnp.floor(jnp.maximum(jnp.minimum(room, own_score), 0.0) * (1.0 / LN2))
-    return own_score - k * LN2, k
-
-
-def fill_rows(own, xi, yi):
-    for ref, lo in ((xi, 0), (yi, W)):
-        feat = own[lo : lo + W, :]
-        shift, _ = row_shift(self_scores(feat))
-        one = shift.astype(BF16).astype(F32)
-        two = (shift - one).astype(BF16).astype(F32)
-        three = shift - one - two
-        at = lax.broadcasted_iota(jnp.int32, (16, OWN), 0)
-        rest = jnp.where(at == 0, -one, jnp.where(at == 1, -two, jnp.where(at == 2, -three, jnp.where(at == 3, 1.0, 0.0))))
-        ref[0:W, :] = feat * jnp.asarray(0.125, BF16)
-        ref[W : W + 16, :] = rest.astype(BF16)
-        ref[W + 16 :, :] = jnp.zeros((128 - W - 16, OWN), BF16)
+    k = jnp.floor(jnp.maximum(jnp.minimum(room, own_score), 0.0) * LOG2E)
+    return own_score * LOG2E - k, k
+
+
+def fill_rows(own, xi, yi, shifts):
+    zero = jnp.zeros((W, OWN), BF16)
+    xi[0:W, :] = own[0:W, :] * jnp.asarray(0.125, BF16)
+    xi[W:, :] = zero
+    yi[0:W, :] = zero
+    yi[W:, :] = own[W:, :] * jnp.asarray(0.125, BF16)
+    shifts[0:1, :] = row_shift(self_scores(own[0:W, :]))[0]
+    shifts[1:2, :] = row_shift(self_scores(own[W:, :]))[0]
 
 
 def own_live(n, d):
@@ -350,58 +337,69 @@
         tile(pl.multiple_of(full * 1024, 1024), 256)
 
 
-def sums_kernel(feats, out, own, xa, ya, xi, yi, sums):
+def sums_kernel(feats, out, own, xi, yi, shifts, acc_t, acc_s):
     doc, _, _, z, _ = coords()
-    d = z * 2 + doc
+    d = doc * 4 + z
     n = live_count(feats)
-    fill_columns(feats, n, xa, ya)
     own_rows(feats, d, own)
-    fill_rows(own, xi, yi)
-    sums[...] = jnp.ones_like(sums)
-    steps = (n + BJ - 1) // BJ
+    fill_rows(own, xi, yi, shifts)
+    acc_t[...] = jnp.ones_like(acc_t)
+    acc_s[...] = jnp.ones_like(acc_s)
+    steps = n // BJ
 
     def tile(start, width):
         at = pl.ds(start, width)
 
-        def step(j, carry):
-            js = pl.ds(pl.multiple_of(j * BJ, BJ), BJ)
-            t = jnp.exp(jnp.dot(xa[js, :], xi[:, at], preferred_element_type=F32))
-            s = jnp.exp(jnp.dot(ya[js, :], yi[:, at], preferred_element_type=F32))
+        def step(j, carry, mask=False):
+            t = jnp.exp2(tile_scores(feats, j, xi[:, at]) * LOG2E - shifts[0:1, at])
+            s = jnp.exp2(tile_scores(feats, j, yi[:, at]) * LOG2E - shifts[1:2, at])
+            if mask:
+                alive = lax.broadcasted_iota(jnp.int32, (BJ, width), 0) + j * BJ < n
+                t = jnp.where(alive, t, 0.0)
+                s = jnp.where(alive, s, 0.0)
             add_t = jnp.sum(t.reshape(BJ // 8, 8, width), axis=0)
             add_s = jnp.sum(s.reshape(BJ // 8, 8, width), axis=0)
             return carry[0] + add_t, carry[1] + add_s
 
         zero = jnp.zeros((8, width), F32)
         t, s = lax.fori_loop(0, steps, step, (zero, zero))
-        sums[0:1, at] = jnp.sum(t, axis=0, keepdims=True)
-        sums[1:2, at] = jnp.sum(s, axis=0, keepdims=True)
+        acc_t[:, at] = t
+        acc_s[:, at] = s
+
+        @pl.when(steps * BJ < n)
+        def _():
+            t, s = step(steps, (acc_t[:, at], acc_s[:, at]), True)
+            acc_t[:, at] = t
+            acc_s[:, at] = s
 
     row_tiles(n, d, tile)
     live = own_live(n, d)
     st = self_scores(own[0:W, :])
     ss = self_scores(own[W:, :])
-    lt = row_shift(st)[0] + jnp.log(sums[0:1, :])
-    ls = row_shift(ss)[0] + jnp.log(sums[1:2, :])
+    lt = shifts[0:1, :] * LN2 + jnp.log(jnp.sum(acc_t[...], axis=0, keepdims=True))
+    ls = shifts[1:2, :] * LN2 + jnp.log(jnp.sum(acc_s[...], axis=0, keepdims=True))
     top = jnp.max(jnp.where(live, jnp.maximum(st, ss), 0.0))
-    out[0:1, :] = jnp.where(live, lt, 0.0)
-    out[1:2, :] = jnp.where(live, ls, 0.0)
-    out[2:3, :] = jnp.full((1, OWN), top)
-    out[3:4, :] = jnp.full((1, OWN), n.astype(F32))
-    out[4:8, :] = jnp.zeros((4, OWN), F32)
+    lt = jnp.where(live, lt, 0.0)
+    ls = jnp.where(live, ls, 0.0)
+    for m in range(16):
+        out[m : m + 1, :] = lt[:, m * 128 : (m + 1) * 128]
+        out[16 + m : 17 + m, :] = ls[:, m * 128 : (m + 1) * 128]
+    at = lax.broadcasted_iota(jnp.int32, (8, 128), 0)
+    out[32:40, :] = jnp.where(at == 0, top, jnp.where(at == 1, n.astype(F32), 0.0))
 
 
 def sums(feats):
     return pl.pallas_call(
         sums_kernel,
-        out_shape=jax.ShapeDtypeStruct((8, OWN), F32),
+        out_shape=jax.ShapeDtypeStruct((40, 128), F32),
         in_specs=[pl.BlockSpec(memory_space=VMEM)],
         out_specs=pl.BlockSpec(memory_space=VMEM),
         scratch_shapes=[
             VMEM((128, OWN), BF16),
-            VMEM((LEN, 128), BF16),
-            VMEM((LEN, 128), BF16),
             VMEM((128, OWN), BF16),
             VMEM((128, OWN), BF16),
+            VMEM((8, OWN), F32),
+            VMEM((8, OWN), F32),
             VMEM((8, OWN), F32),
         ],
         compiler_params=params(),
@@ -411,11 +409,11 @@
 def share_kernel(mine, out, s_own, send, recv):
     doc, head, x, z, yh = coords()
     me = device(doc, head, x, z, yh)
-    d = z * 2 + doc
+    d = doc * 4 + z
     peers = []
     for step in range(1, 8):
         p = (d + step) % 8
-        peers.append(device(p % 2, head, x, p // 2, yh))
+        peers.append(device(p // 4, head, x, p % 4, yh))
     greet(peers, me)
     copies = []
     for step in range(1, 8):
@@ -440,7 +438,7 @@
     vmem = pl.BlockSpec(memory_space=VMEM)
     return pl.pallas_call(
         share_kernel,
-        out_shape=jax.ShapeDtypeStruct((8, 8, OWN), F32),
+        out_shape=jax.ShapeDtypeStruct((8, 40, 128), F32),
         in_specs=[vmem],
         out_specs=vmem,
         scratch_shapes=[dma, dma((7,)), dma((7,))],
@@ -448,17 +446,16 @@
     )(mine)
 
 
-def grads_kernel(feats, lse, grad, kl, own, xa, ya, xi, yi, vt, vs, ot, os_):
+def grads_kernel(feats, lse, grad, kl, own, xi, yi, shifts, v, ot, os_):
     doc, _, _, z, _ = coords()
-    d = z * 2 + doc
-    n = live_count(feats)
-    fill_columns(feats, n, xa, ya)
+    d = doc * 4 + z
+    n = jnp.max(lse[0, 33:34, :]).astype(jnp.int32)
     own_rows(feats, d, own)
-    fill_rows(own, xi, yi)
+    fill_rows(own, xi, yi, shifts)
     steps = (n + BJ - 1) // BJ
 
     def weigh(b, _):
-        f = feats[b // 8, (b // 2) % 4, b % 2, 0:ROWS, :].T
+        f = block(feats, b).T
         x, y = f[:W, :], f[W:, :]
         yf = y.astype(F32)
         at = pl.ds(pl.multiple_of(b * ROWS, ROWS), ROWS)
@@ -466,17 +463,16 @@
         for q in range(4):
             m = (b * 4 + q) // 8
             dd = (b * 4 + q) % 8
-            ms = pl.ds(pl.multiple_of(m * 128, 128), 128)
-            lt.append(lse[dd, 0:1, ms])
-            ls.append(lse[dd, 1:2, ms])
-        lane = lax.broadcasted_iota(jnp.int32, (1, ROWS), 1) + b * ROWS
-        wt = jnp.where(lane < n, jnp.exp(SHIFT - jnp.concatenate(lt, axis=1)), 0.0)
-        ws = jnp.where(lane < n, jnp.exp(SHIFT - jnp.concatenate(ls, axis=1)), 0.0)
-        vt[0:W, at] = y
-        vt[W : 2 * W, at] = (yf * wt).astype(BF16)
-        vt[2 * W :, at] = x
-        vs[0:W, at] = y
-        vs[W:, at] = (yf * ws).astype(BF16)
+            lt.append(lse[dd, pl.ds(m, 1), :])
+            ls.append(lse[dd, pl.ds(16 + m, 1), :])
+        live = lax.broadcasted_iota(jnp.int32, (1, ROWS), 1) + b * ROWS < n
+        wt = jnp.where(live, jnp.exp(SHIFT - jnp.concatenate(lt, axis=1)), 0.0)
+        ws = jnp.where(live, jnp.exp(SHIFT - jnp.concatenate(ls, axis=1)), 0.0)
+        keep = jnp.where(live, 1.0, 0.0).astype(BF16)
+        v[0:W, at] = x * keep
+        v[W : 2 * W, at] = (yf * wt).astype(BF16)
+        v[2 * W : 3 * W, at] = y * keep
+        v[3 * W :, at] = (yf * ws).astype(BF16)
         return 0
 
     lax.fori_loop(0, steps * (BJ // ROWS), weigh, 0)
@@ -488,10 +484,10 @@
 
         def step(j, _):
             js = pl.ds(pl.multiple_of(j * BJ, BJ), BJ)
-            t = jnp.exp(jnp.dot(xa[js, :], xi[:, at], preferred_element_type=F32)).astype(BF16)
-            s = jnp.exp(jnp.dot(ya[js, :], yi[:, at], preferred_element_type=F32)).astype(BF16)
-            ot[:, at] += jnp.dot(vt[:, js], t, preferred_element_type=F32)
-            os_[:, at] += jnp.dot(vs[:, js], s, preferred_element_type=F32)
+            t = jnp.exp2(tile_scores(feats, j, xi[:, at]) * LOG2E - shifts[0:1, at]).astype(BF16)
+            s = jnp.exp2(tile_scores(feats, j, yi[:, at]) * LOG2E - shifts[1:2, at]).astype(BF16)
+            ot[:, at] += jnp.dot(v[0 : 3 * W, js], t, preferred_element_type=F32)
+            os_[:, at] += jnp.dot(v[2 * W :, js], s, preferred_element_type=F32)
             return 0
 
         lax.fori_loop(0, steps, step, 0)
@@ -500,21 +496,22 @@
     live = own_live(n, d)
     x = own[0:W, :].astype(F32)
     y = own[W:, :].astype(F32)
-    lt = lse[d, 0:1, :]
-    ls = lse[d, 1:2, :]
-
-    def finish(acc, feat, l):
+    mine = lse[d]
+    lt = jnp.concatenate([mine[m : m + 1, :] for m in range(16)], axis=1)
+    ls = jnp.concatenate([mine[16 + m : 17 + m, :] for m in range(16)], axis=1)
+
+    def finish(by_row_sum, by_col_sum, feat, l):
         shift, k = row_shift(self_scores(feat))
-        by_row = jnp.exp(shift - l)
-        by_col = jnp.exp((shift - SHIFT) * 0.5)
+        by_row = jnp.exp(shift * LN2 - l)
+        by_col = jnp.exp((shift * LN2 - SHIFT) * 0.5)
         exact = y * jnp.exp(SHIFT - l)
         missing = (exact - exact.astype(BF16).astype(F32)) * jnp.exp2(k)
-        return acc[0:W, :] * by_row + (acc[W : 2 * W, :] + missing) * by_col * by_col, by_row
-
-    gs, _ = finish(os_, own[W:, :], ls)
-    gt, by_row = finish(ot, own[0:W, :], lt)
+        return by_row_sum * by_row + (by_col_sum + missing) * by_col * by_col, by_row
+
+    gs, _ = finish(os_[0:W, :], os_[W:, :], own[W:, :], ls)
+    gt, by_row = finish(ot[2 * W :, :], ot[W : 2 * W, :], own[0:W, :], lt)
     grad[...] = jnp.where(live, (gs - gt) * 0.125, 0.0)
-    moved = jnp.sum(x * ot[2 * W :, :] - y * ot[0:W, :], axis=0, keepdims=True)
+    moved = jnp.sum(x * ot[0:W, :] - y * ot[2 * W :, :], axis=0, keepdims=True)
     rows = jnp.where(live, moved * by_row * 0.125 - lt + ls, 0.0)
     acc = rows[:, 0:128]
     for m in range(1, 16):
@@ -532,12 +529,10 @@
         out_specs=(vmem, vmem),
         scratch_shapes=[
             VMEM((128, OWN), BF16),
-            VMEM((LEN, 128), BF16),
-            VMEM((LEN, 128), BF16),
             VMEM((128, OWN), BF16),
             VMEM((128, OWN), BF16),
-            VMEM((3 * W, LEN), BF16),
-            VMEM((2 * W, LEN), BF16),
+            VMEM((8, OWN), F32),
+            VMEM((4 * W, LEN), BF16),
             VMEM((3 * W, OWN), F32),
             VMEM((2 * W, OWN), F32),
         ],
@@ -547,13 +542,13 @@
 
 def grads_wide(feats, lse):
     doc, _, _, z, _ = coords()
-    d = z * 2 + doc
-    n = lse[0, 3, 0].astype(jnp.int32)
+    d = doc * 4 + z
+    n = lse[0, 33, 0].astype(jnp.int32)
     f = feats[:, :, :, :ROWS, :].reshape(LEN // 1024, 8, 128, 128)
     mine = lax.dynamic_index_in_dim(f, d, 1, keepdims=False).reshape(OWN, 128)
     cols = f.reshape(LEN // 1024, 1024, 128)
-    col_lse = jnp.transpose(lse[:, :2].reshape(8, 2, 16, 128), (2, 1, 0, 3)).reshape(16, 2, 1024)
-    own_lse = lax.dynamic_index_in_dim(lse, d, 0, keepdims=False)
+    col_lse = jnp.transpose(lse[:, :32].reshape(8, 2, 16, 128), (2, 1, 0, 3)).reshape(16, 2, 1024)
+    own_lse = lax.dynamic_index_in_dim(lse, d, 0, keepdims=False)[:32].reshape(2, OWN)
     lt, ls = own_lse[0][:, None], own_lse[1][:, None]
     lane = jnp.arange(OWN)
     live = (((lane // 128) * 8 + d) * 128 + lane % 128 < n)[:, None]
@@ -581,19 +576,14 @@
     return grad.T, tile
 
 
-def give_kernel(grad, kl, gq, gv, loss, got, got_kl, sums, got_sum, sg, rg, sk, rk, ss, rs):
+def give_kernel(grad, kl, got, loss, got_kl, sums, got_sum, sg, rg, sk, rk, ss, rs):
     doc, head, x, z, yh = coords()
     me = device(doc, head, x, z, yh)
-    d = z * 2 + doc
-    to = [device(x // 2, head, m // 4, m % 4, z // 2) for m in range(16)]
-    sources = []
-    for k in range(2):
-        for e in range(2):
-            for q in range(4):
-                sources.append(device(q % 2, head, 2 * doc + k, 2 * yh + q // 2, e))
+    to = [device(x // 2, head, m // 4, m % 4, doc) for m in range(16)]
+    sources = [device(yh, head, 2 * doc + k, q, e) for k in range(2) for e in range(2) for q in range(4)]
     ring = [device(doc, 1 - head, x, z, yh), device(doc, head, x, z, 1 - yh), device(doc, 1 - head, x, z, 1 - yh)]
     greet(to + sources + ring, me)
-    kind, part, q = x % 2, yh, d % 4
+    kind, part, q = x % 2, yh, z
     slot = (kind * 2 + part) * 4 + q
     where = pl.ds(pl.multiple_of(part * W, W), W)
     for m in range(16):
@@ -626,12 +616,6 @@
         )
         copy.start()
         swaps.append(copy)
-    for k, out in ((0, gq), (1, gv)):
-        for q_ in range(4):
-            for e in range(2):
-                part_ref = got.at[k, q_, pl.ds(e * W, W)]
-                pltpu.make_async_copy(part_ref, part_ref, rg.at[(k * 2 + e) * 4 + q_]).wait()
-            out[q_ * 128 : (q_ + 1) * 128, :] = got[k, q_].T
     for i in range(3):
         swaps[i].wait_recv()
         total = total + got_sum[i]
@@ -640,6 +624,11 @@
     kl_sum = jnp.sum(total[0:1, :], axis=1, keepdims=True)
     count = total[1:2, 0:1] * (1.0 / 64.0)
     loss[...] = jnp.broadcast_to(kl_sum / (count * (2.0 * REL_HEADS)), (8, 128))
+    for k in range(2):
+        for q_ in range(4):
+            for e in range(2):
+                part_ref = got.at[k, q_, pl.ds(e * W, W)]
+                pltpu.make_async_copy(part_ref, part_ref, rg.at[(k * 2 + e) * 4 + q_]).wait()
     for m in range(16):
         src = grad.at[:, m * 128 : (m + 1) * 128]
 
@@ -656,14 +645,12 @@
 def give(grad, kl):
     dma = pltpu.SemaphoreType.DMA
     vmem = pl.BlockSpec(memory_space=VMEM)
-    out = jax.ShapeDtypeStruct((ROWS, 128), F32)
     return pl.pallas_call(
         give_kernel,
-        out_shape=(out, out, jax.ShapeDtypeStruct((8, 128), F32)),
+        out_shape=(jax.ShapeDtypeStruct((2, 4, 128, 128), F32), jax.ShapeDtypeStruct((8, 128), F32)),
         in_specs=[vmem, vmem],
-        out_specs=(vmem, vmem, vmem),
+        out_specs=(vmem, vmem),
         scratch_shapes=[
-            VMEM((2, 4, 128, 128), F32),
             VMEM((16, 8, 128), F32),
             VMEM((8, 128), F32),
             VMEM((3, 8, 128), F32),
@@ -673,6 +660,25 @@
     )(grad, kl)
 
 
+def turn_kernel(got, tile, gq, gv, loss):
+    for k, out in ((0, gq), (1, gv)):
+        for q in range(4):
+            out[0, q * 128 : (q + 1) * 128, :] = got[k, q].T
+    loss[0] = jnp.max(tile[...])
+
+
+def turn(got, tile):
+    vmem = pl.BlockSpec(memory_space=VMEM)
+    out = jax.ShapeDtypeStruct((1, ROWS, 128), F32)
+    return pl.pallas_call(
+        turn_kernel,
+        out_shape=(out, out, jax.ShapeDtypeStruct((1,), F32)),
+        in_specs=[vmem, vmem],
+        out_specs=(vmem, vmem, pl.BlockSpec(memory_space=pltpu.SMEM)),
+        compiler_params=params(),
+    )(got, tile)
+
+
 def shards(token_ids, teacher_query, teacher_value, student_query, student_value, teacher_pick, student_pick):
     msg_a, msg_b = pick(
         teacher_pick, student_pick, token_ids.reshape(4, 128),
@@ -680,10 +686,9 @@
     )
     feats = gather(teacher_pick, msg_a, msg_b)
     lse = share(sums(feats))
-    fast = jnp.max(lse[:, 2, 0]) <= FAST_TOP
+    fast = jnp.max(lse[:, 32, 0]) <= FAST_TOP
     grad, kl = lax.cond(fast, grads, grads_wide, feats, lse)
-    gq, gv, loss = give(grad, kl)
-    return gq[None], gv[None], loss[0, :1]
+    return turn(*give(grad, kl))
 
 
 def solution(mesh):

time: 213 us -> 144 us (0.68)
  Pallas kernels: 204 us -> 138 us
  local copies, waits for them, and re-layouts: 6.49 us -> 1.97 us
    pallas_call x3 -> x4, Pallas kernels: 130 us -> 54.7 us  [the longest x1 25.6 us: sums(): pl.pallas_call(sums_kernel, out_shape=jax.ShapeDtypeStruct((40, 128), F32...]
    pallas_call x1, Pallas kernels: 34.1 us -> 42.1 us  [grads(): pl.pallas_call(grads_kernel, out_shape=(jax.ShapeDtypeStruct((W, OWN), F3...]
    unnamed x4 -> x2, local copies, waits for them, and re-layouts: 5.3 us -> 1.97 us
where the time goes in v2:
time: 144 us; the launch traced here: 142 us
  Pallas kernels  138 us (96%)
  local copies, waits for them, and re-layouts  1.97 us (1%)
  between operations  1.49 us (1%)
    pallas_call x1, Pallas kernels, grads(): pl.pallas_call(grads_kernel, out_shape=(jax.ShapeDtypeStruct((W, OWN), F3...  42.1 us
    pallas_call x1, Pallas kernels, gather(): pl.pallas_call(gather_kernel, out_shape=jax.ShapeDtypeStruct((4, 4, 2, PI...  36.8 us
    pallas_call x1, Pallas kernels, sums(): pl.pallas_call(sums_kernel, out_shape=jax.ShapeDtypeStruct((40, 128), F32...  25.6 us
    pallas_call x1, Pallas kernels, give(): pl.pallas_call(give_kernel, out_shape=(jax.ShapeDtypeStruct((2, 4, 128, 1...  19.9 us
    pallas_call x1, Pallas kernels, share(): pl.pallas_call(share_kernel, out_shape=jax.ShapeDtypeStruct((8, 40, 128),...  7.16 us
    pallas_call x1, Pallas kernels, pick(): pl.pallas_call(pick_kernel, out_shape=(jax.ShapeDtypeStruct((2, 2, PIECE,...  4.54 us

profile of v2, /device:TPU:0, one launch (start us, length us, event | category | flops | bytes accessed | tf_op | source)
XLA Modules:
  0.0 142.3 jit_solution(6329506344520946684)
XLA Ops:
  0.6 4.5 %shard_map.94 = (bf16[2,2,528,128]{3,2,1,0:T(8,128)(2,1)}, bf16[2,2,256,128]{3,2,1,0:T(8,128)(2,1)}) custom-call(s32[4]{0:T(128)} %tp.3, s32[4]{0:T(128)} %sp.1, s32[4,128]{1,0:T(4,128)} %bitcast.101, bf16[512,4096]{1,0:T(8,128)(2,1)} %bitcast.84, bf16[512,512]{1,0:T(8,128)(2,1)} %bitcast.89, bf16[512,3584]{1,0:T(8,128)(2,1)} %bitcast.85, ...), custom_call_target="tpu_custom_call" | custom-call | tf_op jit(solution)/shard_map/pallas_call | solution.py:98
  5.2 36.8 %shard_map.95.feats = bf16[4,4,2,528,128]{4,3,2,1,0:T(8,128)(2,1)S(1)} custom-call(s32[4]{0:T(128)} %tp.3, bf16[2,2,528,128]{3,2,1,0:T(8,128)(2,1)} %get-tuple-element.191.msg_a, bf16[2,2,256,128]{3,2,1,0:T(8,128)(2,1)} %get-tuple-element.192.msg_b), custom_call_target="tpu_custom_call" | custom-call | tf_op jit(solution)/shard_map/pallas_call | solution.py:245
  42.0 0.0 copy-start
  42.0 2.0 %copy-done = bf16[4,4,2,528,128]{4,3,2,1,0:T(8,128)(2,1)} copy-done((bf16[4,4,2,528,128]{4,3,2,1,0:T(8,128)(2,1)}, bf16[4,4,2,528,128]{4,3,2,1,0:T(8,128)(2,1)S(1)}, u32[]{:S(2)}) %copy-start) | copy-done | bytes 4325400
  43.9 25.6 %shard_map.96.mine = f32[40,128]{1,0:T(8,128)} custom-call(bf16[4,4,2,528,128]{4,3,2,1,0:T(8,128)(2,1)S(1)} %shard_map.95.feats), custom_call_target="tpu_custom_call" | custom-call | tf_op jit(solution)/shard_map/pallas_call | solution.py:392
  69.6 7.2 %shard_map.97 = f32[8,40,128]{2,1,0:T(8,128)S(1)} custom-call(f32[40,128]{1,0:T(8,128)} %shard_map.96.mine), custom_call_target="tpu_custom_call" | custom-call | tf_op jit(solution)/shard_map/pallas_call | solution.py:439
  76.7 0.6 slice_reduce_fusion
  78.0 42.3 %conditional.1 = ((f32[64,2048]{1,0:T(8,128)S(1)}, f32[8,128]{1,0:T(8,128)S(1)})) conditional(s32[]{:T(128)} %convert_element_type.19, (bf16[4,4,2,528,128]{4,3,2,1,0:T(8,128)(2,1)}, f32[8,40,128]{2,1,0:T(8,128)S(1)}) %tuple.61, (bf16[4,4,2,528,128]{4,3,2,1,0:T(8,128)(2,1)}, f32[8,40,128]{2,1,0:T(8,128)S(1)}) %tuple.62), branch_computations={%region_1.6_spmd, %region_6.7_spmd} | conditional | flops 851920832 | bytes 72522712 | solution.py:690
  78.2 42.1 %branch_1_fun.1 = (f32[64,2048]{1,0:T(8,128)S(1)}, f32[8,128]{1,0:T(8,128)S(1)}) custom-call(bf16[4,4,2,528,128]{4,3,2,1,0:T(8,128)(2,1)} %get-tuple-element.180.feats, f32[8,40,128]{2,1,0:T(8,128)S(1)} %get-tuple-element.181.lse), custom_call_target="tpu_custom_call" | custom-call | tf_op jit(solution)/shard_map/cond/branch_1_fun/pallas_call | solution.py:525
  120.2 19.9 %shard_map.98 = (f32[2,4,128,128]{3,2,1,0:T(8,128)}, f32[8,128]{1,0:T(8,128)}) custom-call(f32[64,2048]{1,0:T(8,128)S(1)} %get-tuple-element.193.grad, f32[8,128]{1,0:T(8,128)S(1)} %get-tuple-element.194.kl), custom_call_target="tpu_custom_call" | custom-call | tf_op jit(solution)/shard_map/pallas_call | solution.py:648
  140.1 2.0 %shard_map.99 = (f32[1,512,128]{2,1,0:T(8,128)}, f32[1,512,128]{2,1,0:T(8,128)}, f32[1]{0:T(128)}) custom-call(f32[2,4,128,128]{3,2,1,0:T(8,128)} %get-tuple-element.195.got, f32[8,128]{1,0:T(8,128)} %get-tuple-element.196.tile), custom_call_target="tpu_custom_call" | custom-call | tf_op jit(solution)/shard_map/pallas_call | solution.py:673
Async XLA Ops:
  42.0 2.0 %copy-start = (bf16[4,4,2,528,128]{4,3,2,1,0:T(8,128)(2,1)}, bf16[4,4,2,528,128]{4,3,2,1,0:T(8,128)(2,1)S(1)}, u32[]{:S(2)}) copy-start(bf16[4,4,2,528,128]{4,3,2,1,0:T(8,128)(2,1)S(1)} %shard_map.95.feats) | copy-start | bytes 12976132
